TPU v7x, 32 devices: a whole 2x2x4 slice. The times are simulated.
32 devices in a mesh: section: 4 (over y, core), tensor: 4 (over z), dp: 2 (over x).
Axes of the slice: x: 2, y: 2, z: 4, core: 2. Of those that a mesh axis runs over, the one named last changes fastest.
Arguments:
- hidden: bfloat16 [64, 8192], P(('section', 'dp'), 'tensor'), may hold values from -250 to 250
- vocab_weight: bfloat16 [8192, 10240], P(None, ('section', 'tensor')), may hold values from -0.6 to 0.6
- target_ids: int32 [64], P(('section', 'dp')), may hold values from 0 to 10239
- ref_logp: float32 [64], P(('section', 'dp')), may hold values from -8 to -0.5
- response_lengths: int32 [8], P(('section', 'dp')), may hold values from 1 to 8
Outputs:
- token_logp: float32 [64], P(('section', 'dp'))
- entropy: float32 [64], P(('section', 'dp'))
- kl_term: float32 [64], P(('section', 'dp'))
All inputs are finite; a program needn't handle non-finite values.
Results may differ from a plain program's by a relative error of at most 0.0015.
Values may be sent and summed in bfloat16 or wider, within the bound.
A program may use at most 64 MiB of HBM per device.

v0:
```python
import jax
import jax.numpy as jnp
from jax import lax
from jax.sharding import PartitionSpec as P


def joined(part, axis, combine):
    gathered = jax.tree.map(lambda a: lax.all_gather(a, axis), part)

    def take(source):
        return jax.tree.map(lambda a: lax.dynamic_index_in_dim(a, source, 0, False), gathered)

    return lax.fori_loop(
        1, lax.axis_size(axis), lambda source, state: combine(state, take(source)), take(0)
    )


def combine(first, second):
    top = jnp.maximum(first[0], second[0])
    left = jnp.exp(first[0] - top)
    right = jnp.exp(second[0] - top)
    return (
        top,
        first[1] * left + second[1] * right,
        first[2] * left + second[2] * right,
        first[3] + second[3],
    )


def per_device(hidden, vocab_weight, target_ids, ref_logp, response_lengths):
    row_dev = hidden.shape[0]
    voc_dev = vocab_weight.shape[1]
    whole = lax.all_gather(hidden, "tensor", axis=1, tiled=True)
    logits = jnp.dot(
        lax.all_gather(whole, "section", axis=0, tiled=True),
        vocab_weight,
        preferred_element_type=jnp.float32,
    )
    all_ids = lax.all_gather(target_ids, "section", axis=0, tiled=True)
    offset = (
        lax.axis_index("section") * lax.axis_size("tensor") + lax.axis_index("tensor")
    ) * voc_dev
    top = jnp.max(logits, axis=1)
    expo = jnp.exp(logits - top[:, None])
    total = jnp.sum(expo, axis=1)
    moment = jnp.sum(expo * logits, axis=1)
    column = offset + jnp.arange(voc_dev, dtype=jnp.int32)
    picked = jnp.sum(jnp.where(all_ids[:, None] == column[None, :], logits, 0.0), axis=1)
    merged = joined((top, total, moment, picked), ("section", "tensor"), combine)
    begin = lax.axis_index("section") * row_dev
    top_own, total_own, moment_own, picked_own = [
        lax.dynamic_slice_in_dim(item, begin, row_dev, 0) for item in merged
    ]
    lse = top_own + jnp.log(total_own)
    logp = picked_own - lse
    ent = lse - moment_own / total_own
    slot = jnp.arange(row_dev, dtype=jnp.int32)
    live = (slot < response_lengths[0]).astype(jnp.float32)
    return (logp * live, ent * live, (logp - ref_logp) * live)


def solution(mesh):
    in_specs = (
        P(("section", "dp"), "tensor"),
        P(None, ("section", "tensor")),
        P(("section", "dp")),
        P(("section", "dp")),
        P(("section", "dp")),
    )
    out_specs = (P(("section", "dp")), P(("section", "dp")), P(("section", "dp")))
    return jax.shard_map(
        per_device, mesh=mesh, in_specs=in_specs, out_specs=out_specs, check_vma=False
    )
```

profile of v0, /device:TPU:0, one launch (start us, length us, event | category | flops | bytes accessed | tf_op | source)
XLA Modules:
  0.0 74.3 jit_solution(191539152687031463)
XLA Ops:
  0.6 0.0 copy-start.3
  0.6 0.0 copy-start.2
  0.7 0.0 copy-start.1
  1.3 15.3 %all_gather.33 = bf16[8,8192]{1,0:T(8,128)(2,1)S(1)} all-gather(bf16[8,2048]{1,0:T(8,128)(2,1)} %param.7), channel_id=1, replica_groups=mesh['section'=4,'tensor'=4,'dp'=2] {'tensor'}, dimensions={1}, use_global_device_ids=true | all-gather | bytes 163840 | tf_op jit(solution)/shard_map/all_gather | solution.py:33
  16.6 0.0 copy-start
  16.6 7.3 %all_gather.34 = bf16[32,8192]{1,0:T(8,128)(2,1)S(1)} all-gather(bf16[8,8192]{1,0:T(8,128)(2,1)S(1)} %all_gather.33), channel_id=1, replica_groups=mesh['section'=4,'tensor'=4,'dp'=2] {'section'}, dimensions={0}, use_global_device_ids=true | all-gather | bytes 655360 | tf_op jit(solution)/shard_map/all_gather | solution.py:35
  23.9 5.8 %fusion.13 = (f32[32]{0:T(128)S(1)}, f32[32,640]{1,0:T(8,128)S(1)}) fusion(bf16[32,8192]{1,0:T(8,128)(2,1)S(1)} %all_gather.34, bf16[8192,640]{1,0:T(8,128)(2,1)} %param.8), kind=kOutput, calls=%fused_computation.27 | convolution fusion | flops 335564768 | bytes 11092096 | tf_op jit(solution)/shard_map/dot_general | solution.py:34
  29.7 0.0 copy-done.3
  29.8 0.6 dynamic-slice
  31.0 0.2 dynamic-update-slice
  31.3 0.0 copy-done.2
  31.3 0.6 dynamic-slice.3
  32.5 0.0 copy-done.1
  32.5 0.2 dynamic-update-slice.3
  32.8 4.3 %all-reduce.3 = s32[32]{0:T(128)S(1)} all-reduce(s32[32]{0:T(128)S(1)} %dynamic-update-slice.3), channel_id=1, replica_groups=mesh['section'=4,'tensor'=4,'dp'=2] {'section'}, use_global_device_ids=true, to_apply=%add.3 | all-reduce | flops 32 | bytes 256
  37.0 0.2 multiply_reduce_fusion
  37.3 0.2 dynamic-update-slice.1
  37.5 0.2 dynamic-update-slice.2
  37.7 0.2 dynamic-update-slice.4
  37.9 33.7 %all-reduce.5 = (f32[512]{0:T(512)S(1)}, f32[512]{0:T(512)S(1)}, f32[512]{0:T(512)S(1)}, f32[512]{0:T(512)S(1)}) all-reduce(f32[512]{0:T(512)S(1)} %dynamic-update-slice, f32[512]{0:T(512)S(1)} %dynamic-update-slice.1, f32[512]{0:T(512)S(1)} %dynamic-update-slice.2, ...), channel_id=2, replica_groups=mesh['section'=4,'tensor'=4,'dp'=2] {'section','tensor'}, use_global_device_ids=true, to_apply=%add | all-reduce | flops 2048 | bytes 16384
  71.7 0.1 reshape.12
  71.7 0.1 reshape.13
  71.8 0.1 reshape.14
  71.9 0.1 reshape.15
  72.0 1.2 %while.21 = (s32[]{:T(128)}, f32[32]{0:T(128)S(1)}, f32[32]{0:T(128)S(1)}, f32[32]{0:T(128)S(1)}, f32[32]{0:T(128)S(1)}, /*index=5*/f32[16,32]{1,0:T(8,128)S(1)}...) while((s32[]{:T(128)}, f32[32]{0:T(128)S(1)}, ...), condition=%wide.region_5.6_spmd, body=%wide.region_4.5_spmd.sunk | while | flops 389 | bytes 2343 | solution.py:13
  73.2 0.0 copy-done
  73.2 0.6 subtract_select_fusion
  73.8 0.5 fusion.11
  (55 shorter events, 0.9 us)
Async XLA Ops:
  0.6 29.1 %copy-start.3 = (u32[32]{0:T(128)S(1)}, u32[32]{0:T(128)}, u32[]{:S(2)}) copy-start(u32[32]{0:T(128)} %constant.82) | copy-start | bytes 388
  0.6 30.6 %copy-start.2 = (u32[32]{0:T(128)S(1)}, u32[32]{0:T(128)}, u32[]{:S(2)}) copy-start(u32[32]{0:T(128)} %constant.97) | copy-start | bytes 388
  0.7 31.8 %copy-start.1 = (s32[8]{0:T(128)S(1)}, s32[8]{0:T(128)}, u32[]{:S(2)}) copy-start(s32[8]{0:T(128)} %param.9) | copy-start | bytes 100
  16.6 56.6 %copy-start = (f32[8]{0:T(128)S(1)}, f32[8]{0:T(128)}, u32[]{:S(2)}) copy-start(f32[8]{0:T(128)} %param.10) | copy-start | bytes 100
where the time goes:
time: 74.6 us; the launch traced here: 74.3 us
  blocking collectives  60.6 us (81%)
  matrix products  5.81 us (8%)
  between operations  2.74 us (4%)
  local copies, waits for them, and re-layouts  2.67 us (4%)
  other arithmetic  2.16 us (3%)
    unnamed x2, blocking collectives  38 us
    all_gather x1, blocking collectives, per_device(): whole = lax.all_gather(hidden, 'tensor', axis=1, tiled=True)  15.3 us
    all_gather x1, blocking collectives, per_device(): lax.all_gather(whole, 'section', axis=0, tiled=True)  7.32 us
    dot_general x1, matrix products, per_device(): jnp.dot(lax.all_gather(whole, 'section', axis=0, tiled=True), vocab_weigh...  5.81 us
    unnamed x20, local copies, waits for them, and re-layouts  2.33 us

commit v1 on v0

v1 whole, which is shorter than its diff:
```python
import functools

import jax
import jax.numpy as jnp
from jax import lax
from jax.experimental import pallas as pl
from jax.experimental.pallas import tpu as pltpu
from jax.sharding import PartitionSpec as P

MESH = pl.DeviceIdType.MESH
LANES = 128


def repeat(count, body):
    if count <= 16:
        for i in range(count):
            body(i)
    else:
        lax.fori_loop(0, count, lambda i, _: (body(i), 0)[1], 0)


def kernel(
    sections, tensors, hidden, weight, ids, ref_logp, lengths,
    out_logp, out_ent, out_kl,
    w, g, id_rows, ref_v, len_v, stat, merged,
    w_sem, own_sem, block_recv, a_send, b_send, c_send, id_send, id_recv, s_send, s_recv,
):
    rows, width = hidden.shape
    voc_dev = weight.shape[1]
    pairs = sections // 2
    peers = sections * tensors
    group = LANES // (4 * rows)
    section = lax.axis_index("section")
    tensor = lax.axis_index("tensor")
    core = section % 2
    pair = section // 2
    sibling = section + 1 - 2 * core
    me = section * tensors + tensor

    def nth(j):
        if tensors & (tensors - 1):
            return (tensor + j) % tensors, (tensor + tensors - j) % tensors
        at, bit = tensor, 1
        while bit < tensors:
            if j & bit:
                at = at + bit - 2 * bit * ((tensor // bit) % 2)
            bit *= 2
        return at, at

    loads = []
    for j in range(tensors):
        _, source = nth(j)
        begin = pl.multiple_of(source * width, width)
        loads.append(pltpu.make_async_copy(weight.at[pl.ds(begin, width)], w.at[j], w_sem.at[j]))
        loads[-1].start()
    own = pltpu.make_async_copy(hidden, g.at[tensor, section], own_sem.at[0])
    own_id = pltpu.make_async_copy(ids, id_rows.at[section], own_sem.at[1])
    own_ref = pltpu.make_async_copy(ref_logp, ref_v, own_sem.at[2])
    own_len = pltpu.make_async_copy(lengths, len_v, own_sem.at[3])
    for copy in (own, own_id, own_ref, own_len):
        copy.start()

    barrier = pltpu.get_barrier_semaphore()

    def greet(k):
        other = (me + k + 1) % peers
        pl.semaphore_signal(
            barrier, inc=1, device_id={"section": other // tensors, "tensor": other % tensors},
            device_id_type=MESH,
        )

    repeat(peers - 1, greet)
    pl.semaphore_wait(barrier, peers - 1)

    def block(source, t, s, send, to_section, to_tensor):
        return pltpu.make_async_remote_copy(
            src_ref=source, dst_ref=g.at[t, s], send_sem=send, recv_sem=block_recv.at[t, s],
            device_id={"section": to_section, "tensor": to_tensor}, device_id_type=MESH,
        )

    def copy_a(j):
        return block(hidden, tensor, section, a_send.at[j], section, nth(j)[0])

    def copy_b(j, source, k):
        to = ((pair + k + 1) % pairs) * 2 + core
        return block(source, nth(j)[1], section, b_send.at[j, k], to, tensor)

    def copy_c(j, source, k):
        s = ((pair + k) % pairs) * 2 + core
        return block(source, nth(j)[1], s, c_send.at[j, k], sibling, tensor)

    def arrived(t, s):
        pltpu.make_async_copy(g.at[t, s], g.at[t, s], block_recv.at[t, s]).wait()

    def id_copy(k):
        return pltpu.make_async_remote_copy(
            src_ref=ids, dst_ref=id_rows.at[section], send_sem=id_send.at[k],
            recv_sem=id_recv.at[section],
            device_id={"section": (section + k + 1) % sections}, device_id_type=MESH,
        )

    for j in range(1, tensors):
        copy_a(j).start()
    repeat(pairs - 1, lambda k: copy_b(0, hidden, k).start())
    copy_c(0, hidden, 0).start()
    repeat(sections - 1, lambda k: id_copy(k).start())

    acc = None
    own.wait()

    def forward_own(j):
        t = nth(j)[1]
        arrived(t, section)
        repeat(pairs - 1, lambda k: copy_b(j, g.at[t, section], k).start())
        copy_c(j, g.at[t, section], 0).start()

    def forward_pairs(j):
        t = nth(j)[1]

        def one(k):
            s = ((pair + k + 1) % pairs) * 2 + core
            arrived(t, s)
            copy_c(j, g.at[t, s], k + 1).start()

        repeat(pairs - 1, one)

    def product(j):
        t = nth(j)[1]
        repeat(pairs, lambda k: arrived(t, ((pair + k) % pairs) * 2 + 1 - core))
        loads[j].wait()
        x = g[t].astype(jnp.float32).reshape(sections * rows, width).astype(jnp.bfloat16)
        return jnp.dot(x, w[j], preferred_element_type=jnp.float32)

    forward_pairs(0)
    for j in range(1, tensors):
        forward_own(j)
        forward_pairs(j)
        part = product(j - 1)
        acc = part if acc is None else acc + part
    part = product(tensors - 1)
    logits = part if acc is None else acc + part

    own_id.wait()

    def id_wait(k):
        s = (section + k + 1) % sections
        pltpu.make_async_copy(id_rows.at[s], id_rows.at[s], id_recv.at[s]).wait()

    repeat(sections - 1, id_wait)
    eye = lax.broadcasted_iota(jnp.int32, (rows, rows), 0) == lax.broadcasted_iota(
        jnp.int32, (rows, rows), 1
    )
    columns = []
    for s in range(sections):
        row = jnp.broadcast_to(id_rows[s].astype(jnp.float32), (rows, rows))
        columns.append(jnp.sum(jnp.where(eye, row, 0.0), axis=1, keepdims=True))
    column = jnp.concatenate(columns, axis=0).astype(jnp.int32) - me * voc_dev

    top = jnp.max(logits, axis=1, keepdims=True)
    expo = jnp.exp(logits - top)
    total = jnp.sum(expo, axis=1, keepdims=True)
    moment = jnp.sum(expo * logits, axis=1, keepdims=True)
    at = lax.broadcasted_iota(jnp.int32, logits.shape, 1)
    picked = jnp.sum(jnp.where(at == column, logits, 0.0), axis=1, keepdims=True)

    span = group * rows
    diagonal = lax.broadcasted_iota(jnp.int32, (LANES, LANES), 0) == lax.broadcasted_iota(
        jnp.int32, (LANES, LANES), 1
    )
    for c in range(sections // group):
        piece = jnp.concatenate(
            [item[c * span : (c + 1) * span] for item in (top, total, moment, picked)], axis=0
        )
        stat[c] = jnp.sum(
            jnp.where(diagonal, jnp.broadcast_to(piece, (LANES, LANES)), 0.0), axis=0, keepdims=True
        )

    def stat_copy(k):
        other = (me + k + 1) % peers
        to = other // tensors
        return pltpu.make_async_remote_copy(
            src_ref=stat.at[to // group], dst_ref=merged.at[me], send_sem=s_send.at[k],
            recv_sem=s_recv.at[me],
            device_id={"section": to, "tensor": other % tensors}, device_id_type=MESH,
        )

    repeat(peers - 1, lambda k: stat_copy(k).start())
    merged[me] = stat[section // group]

    for j in range(1, tensors):
        copy_a(j).wait_send()
    for j in range(tensors):
        repeat(pairs - 1, lambda k: copy_b(j, hidden, k).wait_send())
        repeat(pairs, lambda k: copy_c(j, hidden, k).wait_send())
    repeat(sections - 1, lambda k: id_copy(k).wait_send())
    own_ref.wait()
    own_len.wait()

    def stat_wait(k):
        other = (me + k + 1) % peers
        pltpu.make_async_copy(merged.at[other], merged.at[other], s_recv.at[other]).wait()

    repeat(peers - 1, stat_wait)
    every = merged[...].reshape(peers, LANES)
    lane = lax.broadcasted_iota(jnp.int32, (1, LANES), 1)
    best = jnp.max(every, axis=0, keepdims=True)
    scale = jnp.exp(every - best)
    factor = jnp.where(
        lane < 2 * span, pltpu.roll(scale, span, 1),
        jnp.where(lane < 3 * span, pltpu.roll(scale, 2 * span, 1), 1.0),
    )
    result = jnp.where(lane < span, best, jnp.sum(every * factor, axis=0, keepdims=True))
    mine = result
    for k in range(1, group):
        mine = jnp.where(section % group == k, pltpu.roll(result, LANES - k * rows, 1), mine)
    top = mine
    total = pltpu.roll(mine, LANES - span, 1)
    moment = pltpu.roll(mine, LANES - 2 * span, 1)
    picked = pltpu.roll(mine, LANES - 3 * span, 1)
    top, total, moment, picked = [item[:, :rows] for item in (top, total, moment, picked)]
    lse = top + jnp.log(total)
    logp = picked - lse
    ent = lse - moment / total
    live = (lane[:, :rows] < len_v[...]).astype(jnp.float32)
    out_logp[...] = logp * live
    out_ent[...] = ent * live
    out_kl[...] = (logp - ref_v[...]) * live
    repeat(peers - 1, lambda k: stat_copy(k).wait_send())


def per_device(sections, tensors, hidden, weight, ids, ref_logp, lengths):
    rows, width = hidden.shape
    depth, voc_dev = weight.shape
    pairs = sections // 2
    peers = sections * tensors
    chunks = sections * rows * 4 // LANES
    anywhere = pl.BlockSpec(memory_space=pl.ANY)
    dma = pltpu.SemaphoreType.DMA
    outs = pl.pallas_call(
        functools.partial(kernel, sections, tensors),
        out_shape=[jax.ShapeDtypeStruct((1, rows), jnp.float32)] * 3,
        in_specs=[anywhere] * 5,
        out_specs=[pl.BlockSpec(memory_space=pltpu.VMEM)] * 3,
        scratch_shapes=[
            pltpu.VMEM((tensors, width, voc_dev), jnp.bfloat16),
            pltpu.VMEM((tensors, sections, rows, width), jnp.bfloat16),
            pltpu.VMEM((sections, 1, rows), jnp.int32),
            pltpu.VMEM((1, rows), jnp.float32),
            pltpu.VMEM((1, 1), jnp.int32),
            pltpu.VMEM((chunks, 1, LANES), jnp.float32),
            pltpu.VMEM((peers, 1, LANES), jnp.float32),
            dma((tensors,)),
            dma((4,)),
            dma((tensors, sections)),
            dma((tensors,)),
            dma((tensors, pairs)),
            dma((tensors, pairs)),
            dma((sections,)),
            dma((sections,)),
            dma((peers,)),
            dma((peers,)),
        ],
        compiler_params=pltpu.CompilerParams(
            collective_id=0, has_side_effects=True, vmem_limit_bytes=48 * 1024 * 1024
        ),
    )(hidden, weight, ids.reshape(1, rows), ref_logp.reshape(1, rows), lengths.reshape(1, 1))
    return tuple(item.reshape(rows) for item in outs)


def solution(mesh):
    in_specs = (
        P(("section", "dp"), "tensor"),
        P(None, ("section", "tensor")),
        P(("section", "dp")),
        P(("section", "dp")),
        P(("section", "dp")),
    )
    out_specs = (P(("section", "dp")), P(("section", "dp")), P(("section", "dp")))
    return jax.shard_map(
        functools.partial(per_device, mesh.shape["section"], mesh.shape["tensor"]),
        mesh=mesh, in_specs=in_specs, out_specs=out_specs, check_vma=False,
    )
```

time: 74.6 us -> 29.8 us (0.40)
  blocking collectives: 60.6 us -> 0 us
  Pallas kernels: 0 us -> 24.7 us
  matrix products: 5.81 us -> 0 us
  other arithmetic: 2.16 us -> 0 us
  between operations: 2.74 us -> 1.3 us
  local copies, waits for them, and re-layouts: 2.67 us -> 3.6 us
    unnamed x2 -> x0, blocking collectives: 38 us -> none
    pallas_call x0 -> x1, Pallas kernels: none -> 24.7 us  [per_device(): pl.pallas_call(functools.partial(kernel, sections, tensors), out_shape=[j...]
    all_gather x2 -> x0, blocking collectives: 22.6 us -> none  [the longest x1 15.3 us: per_device(): whole = lax.all_gather(hidden, 'tensor', axis=1, tiled=True)]
    dot_general x1 -> x0, matrix products: 5.81 us -> none  [per_device(): jnp.dot(lax.all_gather(whole, 'section', axis=0, tiled=True), vocab_weigh...]
    unnamed x20 -> x9, local copies, waits for them, and re-layouts: 2.33 us -> 3.6 us
    mul x2 -> x0, other arithmetic: 1.12 us -> none  [per_device(): return (logp * live, ent * live, (logp - ref_logp) * live)]
    add x31 -> x0, other arithmetic: 0.81 us -> none  [the longest x15 0.45 us: combine(): first[1] * left + second[1] * right]
where the time goes in v1:
time: 29.8 us; the launch traced here: 29.6 us
  Pallas kernels  24.7 us (83%)
  local copies, waits for them, and re-layouts  3.6 us (12%)
  between operations  1.3 us (4%)
    pallas_call x1, Pallas kernels, per_device(): pl.pallas_call(functools.partial(kernel, sections, tensors), out_shape=[j...  24.7 us
    unnamed x9, local copies, waits for them, and re-layouts  3.6 us

profile of v1, /device:TPU:0, one launch (start us, length us, event | category | flops | bytes accessed | tf_op | source)
XLA Modules:
  0.0 29.6 jit_solution(5487616451850410134)
XLA Ops:
  1.3 0.0 copy-start
  1.3 0.7 %copy-done = bf16[8,2048]{1,0:T(8,128)(2,1)S(1)} copy-done((bf16[8,2048]{1,0:T(8,128)(2,1)S(1)}, bf16[8,2048]{1,0:T(8,128)(2,1)}, u32[]{:S(2)}) %copy-start) | copy-done | bytes 32792
  2.0 0.0 copy-start.1
  2.0 0.7 %copy-done.1 = s32[8]{0:T(128)S(1)} copy-done((s32[8]{0:T(128)S(1)}, s32[8]{0:T(128)}, u32[]{:S(2)}) %copy-start.1) | copy-done | bytes 56
  2.7 0.0 copy-start.2
  2.7 0.7 %copy-done.2 = f32[8]{0:T(128)S(1)} copy-done((f32[8]{0:T(128)S(1)}, f32[8]{0:T(128)}, u32[]{:S(2)}) %copy-start.2) | copy-done | bytes 56
  3.3 24.7 %shard_map.76 = (f32[1,8]{1,0:T(1,128)S(1)}, f32[1,8]{1,0:T(1,128)S(1)}, f32[1,8]{1,0:T(1,128)S(1)}) custom-call(bf16[8,2048]{1,0:T(8,128)(2,1)S(1)} %copy-done, bf16[8192,640]{1,0:T(8,128)(2,1)} %weight.1, s32[1,8]{1,0:T(1,128)S(1)} %bitcast.7, f32[1,8]{1,0:T(1,128)S(1)} %bitcast.8, s32[1,1]{1,0:T(1,128)} %bitcast.6.lengths), custom_call_target="tpu_custom_call" | custom-call | tf_op jit(solution)/shard_map/pallas_call | solution.py:239
  28.1 0.5 %copy.12 = f32[8]{0:T(128)} copy(f32[8]{0:T(128)S(1)} %bitcast.11) | data formatting | bytes 64
  28.6 0.5 %copy.13 = f32[8]{0:T(128)} copy(f32[8]{0:T(128)S(1)} %bitcast.10) | data formatting | bytes 64
  29.1 0.5 %copy.14 = f32[8]{0:T(128)} copy(f32[8]{0:T(128)S(1)} %bitcast.9) | data formatting | bytes 64
Async XLA Ops:
  1.3 0.8 %copy-start = (bf16[8,2048]{1,0:T(8,128)(2,1)S(1)}, bf16[8,2048]{1,0:T(8,128)(2,1)}, u32[]{:S(2)}) copy-start(bf16[8,2048]{1,0:T(8,128)(2,1)} %hidden.1) | copy-start | bytes 98308
  2.0 0.7 %copy-start.1 = (s32[8]{0:T(128)S(1)}, s32[8]{0:T(128)}, u32[]{:S(2)}) copy-start(s32[8]{0:T(128)} %param.7) | copy-start | bytes 100
  2.7 0.7 %copy-start.2 = (f32[8]{0:T(128)S(1)}, f32[8]{0:T(128)}, u32[]{:S(2)}) copy-start(f32[8]{0:T(128)} %param.8) | copy-start | bytes 100

commit v2 on v1

--- a/solution.py
+++ b/solution.py
@@ -9,6 +9,7 @@
 
 MESH = pl.DeviceIdType.MESH
 LANES = 128
+DIRECT = ()
 
 
 def repeat(count, body):
@@ -83,7 +84,8 @@
 
     def copy_b(j, source, k):
         to = ((pair + k + 1) % pairs) * 2 + core
-        return block(source, nth(j)[1], section, b_send.at[j, k], to, tensor)
+        t, to_tensor = (tensor, nth(j)[0]) if j in DIRECT else (nth(j)[1], tensor)
+        return block(source, t, section, b_send.at[j, k], to, to_tensor)
 
     def copy_c(j, source, k):
         s = ((pair + k) % pairs) * 2 + core
@@ -99,9 +101,11 @@
             device_id={"section": (section + k + 1) % sections}, device_id_type=MESH,
         )
 
+    repeat(pairs - 1, lambda k: copy_b(0, hidden, k).start())
     for j in range(1, tensors):
         copy_a(j).start()
-    repeat(pairs - 1, lambda k: copy_b(0, hidden, k).start())
+    for j in DIRECT:
+        repeat(pairs - 1, lambda k: copy_b(j, hidden, k).start())
     copy_c(0, hidden, 0).start()
     repeat(sections - 1, lambda k: id_copy(k).start())
 
@@ -111,7 +115,8 @@
     def forward_own(j):
         t = nth(j)[1]
         arrived(t, section)
-        repeat(pairs - 1, lambda k: copy_b(j, g.at[t, section], k).start())
+        if j not in DIRECT:
+            repeat(pairs - 1, lambda k: copy_b(j, g.at[t, section], k).start())
         copy_c(j, g.at[t, section], 0).start()
 
     def forward_pairs(j):
@@ -131,14 +136,15 @@
         x = g[t].astype(jnp.float32).reshape(sections * rows, width).astype(jnp.bfloat16)
         return jnp.dot(x, w[j], preferred_element_type=jnp.float32)
 
+    forward_own(1)
     forward_pairs(0)
+    for j in range(2, tensors):
+        forward_own(j)
     for j in range(1, tensors):
-        forward_own(j)
         forward_pairs(j)
         part = product(j - 1)
         acc = part if acc is None else acc + part
-    part = product(tensors - 1)
-    logits = part if acc is None else acc + part
+    logits = acc + product(tensors - 1)
 
     own_id.wait()
 
@@ -234,7 +240,7 @@
     pairs = sections // 2
     peers = sections * tensors
     chunks = sections * rows * 4 // LANES
-    anywhere = pl.BlockSpec(memory_space=pl.ANY)
+    anywhere = pl.BlockSpec(memory_space=pltpu.HBM)
     dma = pltpu.SemaphoreType.DMA
     outs = pl.pallas_call(
         functools.partial(kernel, sections, tensors),

time: 29.8 us -> 25.6 us (0.86)
  Pallas kernels: 24.7 us -> 20.5 us
    pallas_call x1, Pallas kernels: 24.7 us -> 20.5 us  [per_device(): pl.pallas_call(functools.partial(kernel, sections, tensors), out_shape=[j...]
where the time goes in v2:
time: 25.6 us; the launch traced here: 25.4 us
  Pallas kernels  20.5 us (80%)
  local copies, waits for them, and re-layouts  3.6 us (14%)
  between operations  1.3 us (5%)
    pallas_call x1, Pallas kernels, per_device(): pl.pallas_call(functools.partial(kernel, sections, tensors), out_shape=[j...  20.5 us
    unnamed x9, local copies, waits for them, and re-layouts  3.6 us

profile of v2, /device:TPU:0, one launch (start us, length us, event | category | flops | bytes accessed | tf_op | source)
XLA Modules:
  0.0 25.4 jit_solution(8962466007784757261)
XLA Ops:
  1.3 0.0 copy-start
  1.3 0.7 %copy-done = bf16[8,2048]{1,0:T(8,128)(2,1)S(1)} copy-done((bf16[8,2048]{1,0:T(8,128)(2,1)S(1)}, bf16[8,2048]{1,0:T(8,128)(2,1)}, u32[]{:S(2)}) %copy-start) | copy-done | bytes 32792
  2.0 0.0 copy-start.1
  2.0 0.7 %copy-done.1 = s32[8]{0:T(128)S(1)} copy-done((s32[8]{0:T(128)S(1)}, s32[8]{0:T(128)}, u32[]{:S(2)}) %copy-start.1) | copy-done | bytes 56
  2.7 0.0 copy-start.2
  2.7 0.7 %copy-done.2 = f32[8]{0:T(128)S(1)} copy-done((f32[8]{0:T(128)S(1)}, f32[8]{0:T(128)}, u32[]{:S(2)}) %copy-start.2) | copy-done | bytes 56
  3.3 20.5 %shard_map.76 = (f32[1,8]{1,0:T(1,128)S(1)}, f32[1,8]{1,0:T(1,128)S(1)}, f32[1,8]{1,0:T(1,128)S(1)}) custom-call(bf16[8,2048]{1,0:T(8,128)(2,1)S(1)} %copy-done, bf16[8192,640]{1,0:T(8,128)(2,1)} %weight.1, s32[1,8]{1,0:T(1,128)S(1)} %bitcast.7, f32[1,8]{1,0:T(1,128)S(1)} %bitcast.8, s32[1,1]{1,0:T(1,128)} %bitcast.6.lengths), custom_call_target="tpu_custom_call" | custom-call | tf_op jit(solution)/shard_map/pallas_call | solution.py:245
  23.9 0.5 %copy.12 = f32[8]{0:T(128)} copy(f32[8]{0:T(128)S(1)} %bitcast.11) | data formatting | bytes 64
  24.4 0.5 %copy.13 = f32[8]{0:T(128)} copy(f32[8]{0:T(128)S(1)} %bitcast.10) | data formatting | bytes 64
  24.9 0.5 %copy.14 = f32[8]{0:T(128)} copy(f32[8]{0:T(128)S(1)} %bitcast.9) | data formatting | bytes 64
Async XLA Ops:
  1.3 0.8 %copy-start = (bf16[8,2048]{1,0:T(8,128)(2,1)S(1)}, bf16[8,2048]{1,0:T(8,128)(2,1)}, u32[]{:S(2)}) copy-start(bf16[8,2048]{1,0:T(8,128)(2,1)} %hidden.1) | copy-start | bytes 98308
  2.0 0.7 %copy-start.1 = (s32[8]{0:T(128)S(1)}, s32[8]{0:T(128)}, u32[]{:S(2)}) copy-start(s32[8]{0:T(128)} %param.7) | copy-start | bytes 100
  2.7 0.7 %copy-start.2 = (f32[8]{0:T(128)S(1)}, f32[8]{0:T(128)}, u32[]{:S(2)}) copy-start(f32[8]{0:T(128)} %param.8) | copy-start | bytes 100

commit v3 on v1

--- a/solution.py
+++ b/solution.py
@@ -21,7 +21,7 @@
 
 def kernel(
     sections, tensors, hidden, weight, ids, ref_logp, lengths,
-    out_logp, out_ent, out_kl,
+    out,
     w, g, id_rows, ref_v, len_v, stat, merged,
     w_sem, own_sem, block_recv, a_send, b_send, c_send, id_send, id_recv, s_send, s_recv,
 ):
@@ -62,15 +62,14 @@
 
     barrier = pltpu.get_barrier_semaphore()
 
-    def greet(k):
-        other = (me + k + 1) % peers
+    def greet(axis, at, size, k):
         pl.semaphore_signal(
-            barrier, inc=1, device_id={"section": other // tensors, "tensor": other % tensors},
-            device_id_type=MESH,
-        )
-
-    repeat(peers - 1, greet)
-    pl.semaphore_wait(barrier, peers - 1)
+            barrier, inc=1, device_id={axis: (at + k + 1) % size}, device_id_type=MESH
+        )
+
+    repeat(tensors - 1, lambda k: greet("tensor", tensor, tensors, k))
+    repeat(sections - 1, lambda k: greet("section", section, sections, k))
+    pl.semaphore_wait(barrier, tensors + sections - 2)
 
     def block(source, t, s, send, to_section, to_tensor):
         return pltpu.make_async_remote_copy(
@@ -99,13 +98,12 @@
             device_id={"section": (section + k + 1) % sections}, device_id_type=MESH,
         )
 
+    repeat(pairs - 1, lambda k: copy_b(0, hidden, k).start())
     for j in range(1, tensors):
         copy_a(j).start()
-    repeat(pairs - 1, lambda k: copy_b(0, hidden, k).start())
     copy_c(0, hidden, 0).start()
     repeat(sections - 1, lambda k: id_copy(k).start())
 
-    acc = None
     own.wait()
 
     def forward_own(j):
@@ -131,14 +129,16 @@
         x = g[t].astype(jnp.float32).reshape(sections * rows, width).astype(jnp.bfloat16)
         return jnp.dot(x, w[j], preferred_element_type=jnp.float32)
 
+    forward_own(1)
     forward_pairs(0)
-    for j in range(1, tensors):
+    for j in range(2, tensors):
         forward_own(j)
+    logits = product(0)
+    forward_pairs(1)
+    for j in range(2, tensors):
         forward_pairs(j)
-        part = product(j - 1)
-        acc = part if acc is None else acc + part
-    part = product(tensors - 1)
-    logits = part if acc is None else acc + part
+        logits = logits + product(j - 1)
+    logits = logits + product(tensors - 1)
 
     own_id.wait()
 
@@ -222,9 +222,7 @@
     logp = picked - lse
     ent = lse - moment / total
     live = (lane[:, :rows] < len_v[...]).astype(jnp.float32)
-    out_logp[...] = logp * live
-    out_ent[...] = ent * live
-    out_kl[...] = (logp - ref_v[...]) * live
+    out[...] = jnp.concatenate([logp * live, ent * live, (logp - ref_v[...]) * live], axis=0)
     repeat(peers - 1, lambda k: stat_copy(k).wait_send())
 
 
@@ -234,13 +232,13 @@
     pairs = sections // 2
     peers = sections * tensors
     chunks = sections * rows * 4 // LANES
-    anywhere = pl.BlockSpec(memory_space=pl.ANY)
+    anywhere = pl.BlockSpec(memory_space=pltpu.HBM)
     dma = pltpu.SemaphoreType.DMA
     outs = pl.pallas_call(
         functools.partial(kernel, sections, tensors),
-        out_shape=[jax.ShapeDtypeStruct((1, rows), jnp.float32)] * 3,
+        out_shape=jax.ShapeDtypeStruct((3, rows), jnp.float32),
         in_specs=[anywhere] * 5,
-        out_specs=[pl.BlockSpec(memory_space=pltpu.VMEM)] * 3,
+        out_specs=pl.BlockSpec(memory_space=pltpu.VMEM),
         scratch_shapes=[
             pltpu.VMEM((tensors, width, voc_dev), jnp.bfloat16),
             pltpu.VMEM((tensors, sections, rows, width), jnp.bfloat16),
@@ -261,10 +259,10 @@
             dma((peers,)),
         ],
         compiler_params=pltpu.CompilerParams(
-            collective_id=0, has_side_effects=True, vmem_limit_bytes=48 * 1024 * 1024
+            collective_id=0, has_side_effects=True, vmem_limit_bytes=63 * 1024 * 1024
         ),
     )(hidden, weight, ids.reshape(1, rows), ref_logp.reshape(1, rows), lengths.reshape(1, 1))
-    return tuple(item.reshape(rows) for item in outs)
+    return outs[0], outs[1], outs[2]
 
 
 def solution(mesh):

time: 29.8 us -> 22.8 us (0.77)
  Pallas kernels: 24.7 us -> 20.1 us
  local copies, waits for them, and re-layouts: 3.6 us -> 1.3 us
    pallas_call x1, Pallas kernels: 24.7 us -> 20.1 us  [per_device(): pl.pallas_call(functools.partial(kernel, sections, tensors), out_shape=ja...]
    unnamed x9 -> x0, local copies, waits for them, and re-layouts: 3.6 us -> none
    squeeze x0 -> x1, local copies, waits for them, and re-layouts: none -> 1.3 us  [per_device(): return (outs[0], outs[1], outs[2])]
where the time goes in v3:
time: 22.8 us; the launch traced here: 22.7 us
  Pallas kernels  20.1 us (88%)
  local copies, waits for them, and re-layouts  1.3 us (6%)
  between operations  1.29 us (6%)
    pallas_call x1, Pallas kernels, per_device(): pl.pallas_call(functools.partial(kernel, sections, tensors), out_shape=ja...  20.1 us
    squeeze x1, local copies, waits for them, and re-layouts, per_device(): return (outs[0], outs[1], outs[2])  1.3 us

profile of v3, /device:TPU:0, one launch (start us, length us, event | category | flops | bytes accessed | tf_op | source)
XLA Modules:
  0.0 22.7 jit_solution(16979033394401624702)
XLA Ops:
  1.3 20.1 %shard_map.76 = f32[3,8]{1,0:T(4,128)} custom-call(bf16[8,2048]{1,0:T(8,128)(2,1)} %hidden.1, bf16[8192,640]{1,0:T(8,128)(2,1)} %weight.1, s32[1,8]{1,0:T(1,128)} %bitcast.10, f32[1,8]{1,0:T(1,128)} %bitcast.11, s32[1,1]{1,0:T(1,128)} %bitcast.9.lengths), custom_call_target="tpu_custom_call" | custom-call | tf_op jit(solution)/shard_map/pallas_call | solution.py:237
  21.4 1.3 %slice_bitcast_fusion = (f32[8]{0:T(128)}, f32[8]{0:T(128)}, f32[8]{0:T(128)}) fusion(f32[3,8]{1,0:T(4,128)} %shard_map.76), kind=kLoop, calls=%fused_computation | loop fusion | bytes 192 | tf_op jit(solution)/shard_map/squeeze | solution.py:265
